TPU v7x, 128 devices: a whole 4x4x4 slice. The times are simulated.
128 devices in a mesh: date: 16 (over z_hi, x, core), strip: 8 (over z_lo, y).
Axes of the slice: x: 4, y: 4, z: 4 (z_hi: 2, z_lo: 2; z = z_hi * 2 + z_lo), core: 2. Of those that a mesh axis runs over, the one named last changes fastest.
Arguments:
- raw_slc: bfloat16 [128, 512, 2, 3840], P('date', 'strip'), may hold values from -6 to 6
- line_shift: int32 [128], P('date'), may hold values from -1 to 0
- line_phase: int32 [128], P('date'), may hold values from 0 to 15
- col_shift: int32 [128], P('date'), may hold values from -184 to 184
- col_phase: int32 [128], P('date'), may hold values from 0 to 15
- pair_lags: int32 [128, 4], P('date'), may hold values from 0 to 10, as said below
Outputs:
- coherence: float32 [128, 4, 2, 128, 192], P('date', None, None, 'strip')
Inputs may be any that keep to these rules, and one draw needn't show every extreme that they name: `pair_lags`: each date names up to 4 distinct partner distances from 4 to 10, 0 marking an empty slot, with uneven numbers of partners per date; a date plus its distance is always a date of the stack.
All inputs are finite; a program needn't handle non-finite values.
Results may differ from a plain program's by a relative error of at most 0.0067.
Values may be sent and summed in bfloat16 or wider, within the bound.
A program may use at most 192 MiB of HBM per device.

v0:
```python
import jax
import jax.numpy as jnp
from jax import lax
from jax.sharding import PartitionSpec as P

TAPS = 8
PHASES = 16
RBLK = 384
PADC = 192
LOOK_A = 4
LOOK_R = 20
MAXLAG = 10


EPSILON = 1e-06


def padded_2(shard, sides, width):
    for axis, dim in sides:
        peers, length = (lax.axis_size(axis), shard.shape[dim])
        up = [(i, (i + 1) % peers) for i in range(peers - 1)]
        down = [(j, i) for i, j in up]
        last = lax.slice_in_dim(shard, length - width, length, axis=dim)
        initial = lax.slice_in_dim(shard, 0, width, axis=dim)
        before = lax.ppermute(last, axis, up)
        after = lax.ppermute(initial, axis, down)
        shard = jnp.concatenate([before, shard, after], axis=dim)
    return shard


def shifted(block, axis, distance):
    devices = range(lax.axis_size(axis))
    route = [(i - distance, i) for i in devices if i - distance in devices]
    return lax.ppermute(block, axis, route)


def sinc_weights_table():
    phase = jnp.arange(PHASES, dtype=jnp.float32)[:, None] / PHASES
    taps = jnp.arange(TAPS, dtype=jnp.float32)[None, :] - (TAPS // 2 - 1)
    offset = taps - phase
    window = 0.5 + 0.5 * jnp.cos(jnp.pi * offset / (TAPS // 2 + 0.5))
    weights = jnp.sinc(offset) * window
    return (weights / jnp.sum(weights, axis=1, keepdims=True)).astype(jnp.bfloat16)


def pick_weights(sinc_weights, phase_index):
    phase_ids = jnp.arange(PHASES)[:, None]
    return jnp.sum(
        jnp.where(phase_ids == phase_index, sinc_weights.astype(jnp.float32), 0.0), axis=0
    )


def band_from(tap_number, weights):
    tap_ids = jnp.arange(TAPS)
    return jnp.sum(jnp.where(tap_number[..., None] == tap_ids, weights, 0.0), axis=-1).astype(
        jnp.bfloat16
    )


def resample_one(slab, line_off, line_ph, col_off, col_ph, sinc_weights):
    line_count = slab.shape[0] - TAPS
    col_count = slab.shape[2]
    half_taps = TAPS // 2 - 1
    out_rows = jnp.arange(line_count)[:, None]
    src_rows = jnp.arange(line_count + TAPS)[None, :]
    line_taps = src_rows - out_rows - line_off - (TAPS // 2 - half_taps)
    line_matrix = band_from(line_taps, pick_weights(sinc_weights, line_ph))
    azimuth = jnp.dot(
        line_matrix,
        slab.reshape(line_count + TAPS, 2 * col_count),
        preferred_element_type=jnp.float32,
    )
    azimuth = azimuth.astype(jnp.bfloat16).reshape(line_count * 2, col_count)
    padded = jnp.pad(azimuth, ((0, 0), (PADC, PADC)))
    width = RBLK + 2 * PADC
    windows = jnp.stack(
        [
            padded[:, block_index * RBLK : block_index * RBLK + width]
            for block_index in range(col_count // RBLK)
        ]
    )
    src_cols = jnp.arange(width)[:, None]
    out_cols = jnp.arange(RBLK)[None, :]
    col_taps = src_cols - out_cols - PADC - col_off + half_taps
    band_matrix = band_from(col_taps, pick_weights(sinc_weights, col_ph))
    ranged = jnp.einsum("bnw,wr->nbr", windows, band_matrix, preferred_element_type=jnp.float32)
    return (
        ranged.reshape(line_count * 2, col_count)
        .astype(jnp.bfloat16)
        .reshape(line_count, 2, col_count)
    )


def resample_many(extended, line_off, line_ph, col_off, col_ph, sinc_weights):

    def per_member(member):
        return resample_one(member[0], member[1], member[2], member[3], member[4], sinc_weights)

    return lax.map(per_member, (extended, line_off, line_ph, col_off, col_ph))


def on_device(raw_slc, line_shift, line_phase, col_shift, col_phase, pair_lags):
    date_count, line_count, _, col_count = raw_slc.shape
    slot_count = pair_lags.shape[1]
    keep_count = MAXLAG - date_count
    sinc_weights = sinc_weights_table()
    extended = padded_2(raw_slc, (("strip", 1),), TAPS // 2)
    coreg_local = resample_many(
        extended, line_shift, line_phase, col_shift, col_phase, sinc_weights
    )
    neighbour = shifted(coreg_local, "date", -1)
    further = shifted(coreg_local[:keep_count], "date", -2)
    coreg_all = jnp.concatenate([coreg_local, neighbour, further], axis=0)
    look_cols = col_count // LOOK_R
    look_matrix = (
        jnp.arange(col_count)[:, None] // LOOK_R == jnp.arange(look_cols)[None, :]
    ).astype(jnp.bfloat16)

    def looked(stacked):
        count = stacked.shape[0]
        summed = jnp.dot(
            stacked.reshape(count * line_count, col_count),
            look_matrix,
            preferred_element_type=jnp.float32,
        )
        return jnp.sum(summed.reshape(count, line_count // LOOK_A, LOOK_A, look_cols), axis=2)

    def power_of(member):
        values = member.astype(jnp.float32)
        return looked((values[:, 0] ** 2 + values[:, 1] ** 2).astype(jnp.bfloat16)[None])[0]

    power_all = lax.map(power_of, coreg_all)

    def per_pair(pair_index):
        date_index = pair_index // slot_count
        slot_index = pair_index % slot_count
        lag_value = lax.dynamic_index_in_dim(
            lax.dynamic_index_in_dim(pair_lags, date_index, 0, False), slot_index, 0, False
        )
        partner = date_index + jnp.where(lag_value > 0, lag_value, 0)
        ref_float = lax.dynamic_index_in_dim(coreg_all, date_index, 0, False).astype(jnp.float32)
        other_float = lax.dynamic_index_in_dim(coreg_all, partner, 0, False).astype(jnp.float32)
        re_part = ref_float[:, 0] * other_float[:, 0] + ref_float[:, 1] * other_float[:, 1]
        im_part = ref_float[:, 1] * other_float[:, 0] - ref_float[:, 0] * other_float[:, 1]
        looked_sum = looked(jnp.stack([re_part, im_part]).astype(jnp.bfloat16))
        power_ref = lax.dynamic_index_in_dim(power_all, date_index, 0, False)
        power_other = lax.dynamic_index_in_dim(power_all, partner, 0, False)
        scale = jnp.sqrt(power_ref * power_other + EPSILON)
        return jnp.where(lag_value > 0, looked_sum / scale, jnp.zeros_like(looked_sum))

    results = lax.map(per_pair, jnp.arange(date_count * slot_count, dtype=jnp.int32))
    return results.reshape(date_count, slot_count, 2, line_count // LOOK_A, look_cols)


def solution(mesh):
    return jax.shard_map(
        on_device,
        mesh=mesh,
        in_specs=(
            P("date", "strip", None, None),
            P("date"),
            P("date"),
            P("date"),
            P("date"),
            P("date", None),
        ),
        out_specs=P("date", None, None, "strip", None),
        check_vma=False,
    )
```

profile of v0, /device:TPU:36, one launch (start us, length us, event | category | flops | bytes accessed | tf_op | source)
XLA Modules:
  0.0 641.8 jit_solution(1607474389005710191)
XLA Ops:
  0.0 1.9 fusion.109
  1.9 3.5 collective-permute-start
  5.4 4.5 collective-permute-start.1
  10.0 8.8 %collective-permute-done = bf16[8,4,2,3840]{3,2,1,0:T(2,128)(2,1)S(1)} collective-permute-done((bf16[8,4,2,3840]{3,2,1,0:T(2,128)(2,1)S(1)}, bf16[8,4,2,3840]{3,2,1,0:T(2,128)(2,1)S(1)}, u32[]{:S(2)}, u32[]{:S(2)}) %collective-permute-start) | collective-permute-done | bytes 491552 | tf_op jit(solution)/shard_map/ppermute | solution.py:25
  20.0 15.0 %pad_maximum_fusion = bf16[8,72,2,3840]{3,2,1,0:T(2,128)(2,1)} fusion(bf16[8,4,2,3840]{3,2,1,0:T(2,128)(2,1)S(1)} %collective-permute-done.1, bf16[8,64,2,3840]{3,2,1,0:T(2,128)(2,1)} %param.12, bf16[8,4,2,3840]{3,2,1,0:T(2,128)(2,1)S(1)} %collective-permute-done), kind=kLoop, calls=%fused_computation.113 | loop fusion | flops 8847360 | bytes 17694720 | tf_op jit(solution)/shard_map/concatenate | solution.py:27
  35.0 137.9 %while.38 = (s32[]{:T(128)}, bf16[8,64,2,3840]{3,1,2,0:T(8,128)(2,1)}, s32[8]{0:T(128)S(1)}, s32[8]{0:T(128)S(1)}, s32[8]{0:T(128)S(1)}, /*index=5*/s32[8]{0:T(1...) while((s32[]{:T(128)}, ...), condition=%wide.region_6.7_spmd.clone, body=%wide.region_1.6_spmd.clone.sunk | while | flops 834824832 | bytes 26425884 | solution.py:99
  39.8 2.0 constant_dynamic-slice_fusion.2
  43.5 3.4 select_reduce_fusion.5
  57.1 2.0 constant_dynamic-slice_fusion.2
  60.8 3.4 select_reduce_fusion.5
  66.4 1.4 copy.43
  74.3 2.0 constant_dynamic-slice_fusion.2
  78.0 3.4 select_reduce_fusion.5
  91.5 2.0 constant_dynamic-slice_fusion.2
  95.2 3.4 select_reduce_fusion.5
  108.7 2.0 constant_dynamic-slice_fusion.2
  112.5 3.4 select_reduce_fusion.5
  126.0 2.0 constant_dynamic-slice_fusion.2
  129.7 3.4 select_reduce_fusion.5
  143.2 2.0 constant_dynamic-slice_fusion.2
  147.0 3.4 select_reduce_fusion.5
  160.4 2.0 constant_dynamic-slice_fusion.2
  164.2 3.4 select_reduce_fusion.5
  172.9 1.9 collective-permute-start.2
  174.8 2.9 slice.117
  177.7 2.6 collective-permute-start.3
  180.4 7.1 %constant_dynamic-update-slice_fusion.2 = bf16[18,64,2,3840]{3,1,2,0:T(8,128)(2,1)} fusion(bf16[8,64,2,3840]{3,1,2,0:T(8,128)(2,1)} %get-tuple-element.251), kind=kLoop, calls=%fused_computation.132 | loop fusion | bytes 15728640
  187.4 94.1 %collective-permute-done.2 = bf16[8,64,2,3840]{3,1,2,0:T(8,128)(2,1)} collective-permute-done((bf16[8,64,2,3840]{3,1,2,0:T(8,128)(2,1)}, bf16[8,64,2,3840]{3,1,2,0:T(8,128)(2,1)}, u32[]{:S(2)}, u32[]{:S(2)}) %collective-permute-start.2) | collective-permute-done | bytes 7864352 | tf_op jit(solution)/shard_map/ppermute | solution.py:34
  281.5 7.1 %constant_dynamic-update-slice_fusion.1 = bf16[18,64,2,3840]{3,1,2,0:T(8,128)(2,1)} fusion(bf16[18,64,2,3840]{3,1,2,0:T(8,128)(2,1)} %constant_dynamic-update-slice_fusion.2, bf16[8,64,2,3840]{3,1,2,0:T(8,128)(2,1)} %collective-permute-done.2), kind=kLoop, calls=%fused_computation.131 | loop fusion | bytes 15728640
  288.6 15.5 %collective-permute-done.3 = bf16[2,64,2,3840]{3,1,2,0:T(8,128)(2,1)S(1)} collective-permute-done((bf16[2,64,2,3840]{3,1,2,0:T(8,128)(2,1)}, bf16[2,64,2,3840]{3,1,2,0:T(8,128)(2,1)S(1)}, u32[]{:S(2)}, u32[]{:S(2)}) %collective-permute-start.3) | collective-permute-done | bytes 1966112 | tf_op jit(solution)/shard_map/ppermute | solution.py:34
  305.5 40.1 %while.39 = (s32[]{:T(128)}, f32[18,16,192]{2,1,0:T(8,128)S(1)}, bf16[18,64,2,3840]{3,1,2,0:T(8,128)(2,1)}, s32[3840]{0:T(1024)S(1)}, s32[]{:T(128)}) while((s32[]{:T(128)}, f32[18,16,192]{2,1,0:T(8,128)S(1)}, bf16[18,64,2,3840]{3,1,2,0:T(8,128)(2,1)}, s32[3840]{0:T(1024)S(1)}, s32[]{:T(128)}) %tuple.88), condition=%wide.region_9.10_spmd.clone, body=%wide.region_7.9_spmd.clone.sunk | while | flops 97330176 | bytes 6941773 | solution.py:132
  345.6 295.2 %while.40 = (s32[]{:T(128)}, f32[32,2,16,192]{3,2,1,0:T(8,128)S(1)}, s32[32]{0:T(128)S(1)}, s32[8,4]{0,1:T(4,128)}, bf16[18,64,2,3840]{3,1,2,0:T(8,128)(2,1)}, /...) while((s32[]{:T(128)}, ...), condition=%wide.region_12.13_spmd.clone, body=%wide.region_10.12_spmd.clone.sunk | while | flops 193695776 | bytes 15887942 | solution.py:151
  351.8 1.8 bitcast_convert_fusion.6
  361.0 1.8 bitcast_convert_fusion.6
  370.2 1.8 bitcast_convert_fusion.6
  379.4 1.8 bitcast_convert_fusion.6
  388.7 1.8 bitcast_convert_fusion.6
  397.9 1.8 bitcast_convert_fusion.6
  407.1 1.9 bitcast_convert_fusion.6
  416.4 1.9 bitcast_convert_fusion.6
  425.6 1.8 bitcast_convert_fusion.6
  434.9 1.8 bitcast_convert_fusion.6
  444.1 1.8 bitcast_convert_fusion.6
  453.3 1.8 bitcast_convert_fusion.6
  462.5 1.8 bitcast_convert_fusion.6
  471.7 1.8 bitcast_convert_fusion.6
  481.0 1.8 bitcast_convert_fusion.6
  490.2 1.8 bitcast_convert_fusion.6
  499.4 1.8 bitcast_convert_fusion.6
  508.6 1.8 bitcast_convert_fusion.6
  517.9 1.8 bitcast_convert_fusion.6
  527.1 1.8 bitcast_convert_fusion.6
  536.3 1.8 bitcast_convert_fusion.6
  545.5 1.8 bitcast_convert_fusion.6
  554.8 1.8 bitcast_convert_fusion.6
  564.0 1.8 bitcast_convert_fusion.6
  573.3 1.8 bitcast_convert_fusion.6
  582.5 1.8 bitcast_convert_fusion.6
  591.7 1.8 bitcast_convert_fusion.6
  600.9 1.8 bitcast_convert_fusion.6
  610.1 1.8 bitcast_convert_fusion.6
  619.3 1.8 bitcast_convert_fusion.6
  628.5 1.8 bitcast_convert_fusion.6
  637.7 1.8 bitcast_convert_fusion.6
  (637 shorter events, 238.2 us)
Async XLA Ops:
  1.9 17.0 %collective-permute-start = (bf16[8,4,2,3840]{3,2,1,0:T(2,128)(2,1)S(1)}, bf16[8,4,2,3840]{3,2,1,0:T(2,128)(2,1)S(1)}, u32[]{:S(2)}, u32[]{:S(2)}) collective-permute-start(bf16[8,4,2,3840]{3,2,1,0:T(2,128)(2,1)S(1)} %get-tuple-element.357), channel_id=1, source_target_pairs={{0,1},{1,2},{2,3},{3,4},{4,5},{5,6},{6,7},{8,9},{9,10},{10,11},{11... | collective-permute-start | bytes 1474568 | tf_op jit(solution)/shard_map/ppermute | solution.py:25
  5.4 14.7 %collective-permute-start.1 = (bf16[8,4,2,3840]{3,2,1,0:T(2,128)(2,1)S(1)}, bf16[8,4,2,3840]{3,2,1,0:T(2,128)(2,1)S(1)}, u32[]{:S(2)}, u32[]{:S(2)}) collective-permute-start(bf16[8,4,2,3840]{3,2,1,0:T(2,128)(2,1)S(1)} %get-tuple-element.358), channel_id=1, source_target_pairs={{1,0},{2,1},{3,2},{4,3},{5,4},{6,5},{7,6},{9,8},{10,9},{11,10},{12... | collective-permute-start | bytes 1474568 | tf_op jit(solution)/shard_map/ppermute | solution.py:26
  10.0 25.0 %copy-start.1 = (s32[8]{0:T(128)S(1)}, s32[8]{0:T(128)}, u32[]{:S(2)}) copy-start(s32[8]{0:T(128)} %param.15) | copy-start | bytes 100
  10.0 25.0 %copy-start.2 = (s32[8]{0:T(128)S(1)}, s32[8]{0:T(128)}, u32[]{:S(2)}) copy-start(s32[8]{0:T(128)} %param.16) | copy-start | bytes 100
  10.0 25.0 %copy-start.3 = (s32[8]{0:T(128)S(1)}, s32[8]{0:T(128)}, u32[]{:S(2)}) copy-start(s32[8]{0:T(128)} %param.13) | copy-start | bytes 100
  10.0 25.0 %copy-start.4 = (s32[8]{0:T(128)S(1)}, s32[8]{0:T(128)}, u32[]{:S(2)}) copy-start(s32[8]{0:T(128)} %param.14) | copy-start | bytes 100
  172.9 108.6 %collective-permute-start.2 = (bf16[8,64,2,3840]{3,1,2,0:T(8,128)(2,1)}, bf16[8,64,2,3840]{3,1,2,0:T(8,128)(2,1)}, u32[]{:S(2)}, u32[]{:S(2)}) collective-permute-start(bf16[8,64,2,3840]{3,1,2,0:T(8,128)(2,1)} %get-tuple-element.251), channel_id=1, source_target_pairs={{8,0},{16,8},{24,16},{32,24},{40,32},{48,40},{56,48},{64,56},{72,6... | collective-permute-start | bytes 23592968 | tf_op jit(solution)/shard_map/ppermute | solution.py:34
  177.7 126.4 %collective-permute-start.3 = (bf16[2,64,2,3840]{3,1,2,0:T(8,128)(2,1)}, bf16[2,64,2,3840]{3,1,2,0:T(8,128)(2,1)S(1)}, u32[]{:S(2)}, u32[]{:S(2)}) collective-permute-start(bf16[2,64,2,3840]{3,1,2,0:T(8,128)(2,1)} %slice.117), channel_id=1, source_target_pairs={{16,0},{24,8},{32,16},{40,24},{48,32},{56,40},{64,48},{72,56},{80,... | collective-permute-start | bytes 5898248 | tf_op jit(solution)/shard_map/ppermute | solution.py:34
  640.8 1.0 copy-start
where the time goes:
time: 652 us; the launch traced here: 642 us
  local copies, waits for them, and re-layouts  172 us (26%)
  other arithmetic  160 us (25%)
  loops' own time  136 us (21%)
  waiting for transfers between devices  119 us (18%)
  matrix products  42.3 us (6%)
  starting transfers between devices  12.5 us (2%)
    another operation x1, loops' own time, on_device(): lax.map(per_pair, jnp.arange(date_count * slot_count, dtype=jnp.int32))  134 us
    ppermute x2, waiting for transfers between devices, shifted(): return lax.ppermute(block, axis, route)  110 us
    convert_element_type x32, other arithmetic, per_pair(): lax.dynamic_index_in_dim(coreg_all, date_index, 0, False)  58.6 us
    dynamic_slice x32, local copies, waits for them, and re-layouts, per_pair(): lax.dynamic_index_in_dim(lax.dynamic_index_in_dim(pair_lags, date_index,...  42.7 us
    dynamic_slice x40, local copies, waits for them, and re-layouts, resample_many(): return lax.map(per_member, (extended, line_off, line_ph, col_off, col_ph))  35.9 us
    dot_general x50, matrix products, looked(): jnp.dot(stacked.reshape(count * line_count, col_count), look_matrix, pref...  31.2 us
    reduce_sum x16, other arithmetic, band_from(): jnp.sum(jnp.where(tap_number[..., None] == tap_ids, weights, 0.0), axis=-1)  28.3 us
    convert_element_type x18, other arithmetic, power_of(): values = member.astype(jnp.float32)  24 us
  transfers between devices with their start and end apart: 4, of which 4 were waited for; matrix products, arithmetic and copies ran while one was open for 3% of the time, Pallas kernels for 0%

commit v1 on v0

v1 whole, which is shorter than its diff:
```python
import functools

import jax
import jax.numpy as jnp
import numpy as np
from jax import lax
from jax.experimental import pallas as pl
from jax.experimental.pallas import tpu as pltpu
from jax.sharding import PartitionSpec as P

TAPS = 8
PHASES = 16
LOOK_A = 4
LOOK_R = 20
MINLAG = 4
MAXLAG = 10
EPSILON = 1e-06

LAGS = MAXLAG - MINLAG + 1
DATES = 8
LINES = 64
COLS = 3840
TILES = COLS // 128
HALF = COLS // 2
HTILES = HALF // 128
LOOKS = HALF // LOOK_R
LROWS = LINES // LOOK_A
ROWS = 2 * LINES
EDGE = TAPS // 2
SRC = LINES + 2 * EDGE
MOVED = 5
OWN0 = MOVED
NEXT0 = OWN0 + 2 * DATES
IMAGES = NEXT0 + MOVED
UFIRST = MINLAG
UCOUNT = 2 * DATES + MOVED - UFIRST

BF = jnp.bfloat16
F32 = jnp.float32
MESH = pl.DeviceIdType.MESH


def sinc_table():
    phase = np.arange(PHASES)[:, None] / PHASES
    offset = np.arange(TAPS)[None, :] - (TAPS // 2 - 1) - phase
    weights = np.sinc(offset) * (0.5 + 0.5 * np.cos(np.pi * offset / (TAPS // 2 + 0.5)))
    weights = (weights / weights.sum(axis=1, keepdims=True)).astype(np.float32)
    return weights.astype(BF).astype(np.float32).reshape(-1)


def kernel(
    raw, line_shift, line_phase, col_shift, col_phase, lags, table,
    out,
    images, other, halo, src, azim, lhs, look, power, mine, theirs, back, send_back,
    load_sem, halo_send, halo_recv, pair_send, pair_recv, far_send, far_recv,
    res_send, res_recv, back_send, back_recv,
):
    d, s = lax.axis_index("date"), lax.axis_index("strip")
    n_date, n_strip = lax.axis_size("date"), lax.axis_size("strip")
    core = d % 2
    chip = d // 2
    has_next = chip < n_date // 2 - 1
    has_prev = chip > 0
    has_up = s > 0
    has_down = s < n_strip - 1
    partner = d + 1 - 2 * core
    far_ok = jnp.where(core == 0, has_prev, has_next)
    far_chip = jnp.where(core == 0, chip - 1, chip + 1)

    def place(i):
        return jnp.where(core == 0, i, DATES - 1 - i)

    def load_tile(i, slot, c):
        return pltpu.make_async_copy(
            raw.at[place(i), :, :, pl.ds(pl.multiple_of(c * 128, 128), 128)],
            src.at[slot, c, pl.ds(EDGE, LINES)],
            load_sem.at[slot],
        )

    def load_edges(i, slot, c, side):
        return pltpu.make_async_copy(
            halo.at[i, side, :, :, pl.ds(pl.multiple_of(c * 128, 128), 128)],
            src.at[slot, c, pl.ds(side * (EDGE + LINES), EDGE)],
            load_sem.at[slot],
        )

    def start_lines(i, slot):
        @pl.loop(0, TILES)
        def _(c):
            load_tile(i, slot, c).start()

    def start_edges(i, slot):
        @pl.loop(0, TILES)
        def _(c):
            load_edges(i, slot, c, 0).start()
            load_edges(i, slot, c, 1).start()

    start_lines(0, 0)

    barrier = pltpu.get_barrier_semaphore()
    peers = 0
    for step in (-2, -1, 1, 2):
        ok = (d + step >= 0) & (d + step < n_date)
        peers = peers + ok.astype(jnp.int32)

        @pl.when(ok)
        def _():
            pl.semaphore_signal(barrier, inc=1, device_id=(d + step, s), device_id_type=MESH)

    for step, ok in ((-1, has_up), (1, has_down)):
        peers = peers + ok.astype(jnp.int32)

        @pl.when(ok)
        def _():
            pl.semaphore_signal(barrier, inc=1, device_id=(d, s + step), device_id_type=MESH)

    pl.semaphore_wait(barrier, peers)

    def edge_copy(i, side):
        return pltpu.make_async_remote_copy(
            src_ref=raw.at[place(i), pl.ds((1 - side) * (LINES - EDGE), EDGE)],
            dst_ref=halo.at[i, side],
            send_sem=halo_send.at[i, side],
            recv_sem=halo_recv.at[i, side],
            device_id=(d, s + 1 - 2 * side),
            device_id_type=MESH,
        )

    @pl.loop(0, DATES)
    def _(i):
        @pl.when(has_down)
        def _():
            edge_copy(i, 0).start()

        @pl.when(has_up)
        def _():
            edge_copy(i, 1).start()

    @pl.when(jnp.logical_not(has_up))
    def _():
        @pl.loop(0, DATES)
        def _(i):
            halo[i, 0] = jnp.zeros((EDGE, 2, COLS), BF)

    @pl.when(jnp.logical_not(has_down))
    def _():
        @pl.loop(0, DATES)
        def _(i):
            halo[i, 1] = jnp.zeros((EDGE, 2, COLS), BF)

    for t in (0, 1, TILES + 2, TILES + 3, TILES + 4):
        azim[t] = jnp.zeros((ROWS, 128), BF)
    look_row = lax.broadcasted_iota(jnp.int32, (HALF, LOOKS), 0)
    look_col = lax.broadcasted_iota(jnp.int32, (HALF, LOOKS), 1) * LOOK_R
    look[...] = jnp.where(
        (look_row >= look_col) & (look_row < look_col + LOOK_R), 1.0, 0.0
    ).astype(BF)

    def edge_wait(i):
        @pl.when(has_up)
        def _():
            edge_copy(i, 0).wait_recv()

        @pl.when(has_down)
        def _():
            edge_copy(i, 1).wait_recv()

    def far_copy(i, half_own):
        at = jnp.where(core == 0, NEXT0 + i, OWN0 - 1 - i)
        target = 2 * far_chip + (core if half_own else 1 - core)
        return pltpu.make_async_remote_copy(
            src_ref=images.at[OWN0 + DATES * core + place(i)] if half_own else other.at[i],
            dst_ref=images.at[at],
            send_sem=far_send.at[i, 1 if half_own else 0],
            recv_sem=far_recv.at[core, i],
            device_id=(target, s),
            device_id_type=MESH,
        )

    def far_arrived(side, i):
        at = NEXT0 + i if side == 0 else OWN0 - 1 - i
        return pltpu.make_async_remote_copy(
            src_ref=images.at[at], dst_ref=images.at[at],
            send_sem=far_send.at[i, 0], recv_sem=far_recv.at[side, i],
            device_id=(partner, s), device_id_type=MESH,
        )

    def pair_copy(i):
        return pltpu.make_async_remote_copy(
            src_ref=other.at[i],
            dst_ref=images.at[OWN0 + DATES * core + place(i)],
            send_sem=pair_send.at[i],
            recv_sem=pair_recv.at[i],
            device_id=(partner, s),
            device_id_type=MESH,
        )

    out_row = lax.broadcasted_iota(jnp.int32, (ROWS, 2 * SRC), 0)
    src_row = lax.broadcasted_iota(jnp.int32, (ROWS, 2 * SRC), 1)
    within = out_row % LINES
    out_line = (within % LROWS) * LOOK_A + within // LROWS
    line_tap = jnp.where(src_row % 2 == out_row // LINES, src_row // 2 - out_line - 1, 1000)
    col_tap = lax.broadcasted_iota(jnp.int32, (256, 256), 0) - lax.broadcasted_iota(
        jnp.int32, (256, 256), 1
    )

    edge_wait(0)
    start_edges(0, 0)

    @pl.loop(0, DATES)
    def _(i):
        slot = i % 2
        at = place(i)
        pltpu.make_async_copy(
            src.at[slot], src.at[slot], load_sem.at[slot]
        ).wait()

        @pl.when(i < DATES - 1)
        def _():
            start_lines(i + 1, 1 - slot)
            edge_wait(i + 1)
            start_edges(i + 1, 1 - slot)

        line_off, line_ph = line_shift[at], line_phase[at]
        col_off, col_ph = col_shift[at] - (TAPS // 2 - 1) + 256, col_phase[at]
        tile_off, rest = col_off // 128, col_off % 128
        line_band = jnp.zeros((ROWS, 2 * SRC), F32)
        band0 = jnp.zeros((256, 256), F32)
        band1 = jnp.zeros((144, 256), F32)
        for k in range(TAPS):
            line_band = jnp.where(line_tap - line_off == k, table[line_ph * TAPS + k], line_band)
            weight = table[col_ph * TAPS + k]
            band0 = jnp.where(col_tap - rest == k, weight, band0)
            band1 = jnp.where(col_tap[:144] + 256 - rest == k, weight, band1)
        line_band = line_band.astype(BF)
        col_band = jnp.concatenate([band0, band1], axis=0).astype(BF)

        for b in range(TILES // 2):
            block = jnp.concatenate(
                [src.at[slot, 2 * b + j].reshape(2 * SRC, 128)[...] for j in range(2)], axis=1
            )
            got = jnp.dot(line_band, block, preferred_element_type=F32).astype(BF)
            azim[2 * b + 2] = got[:, :128]
            azim[2 * b + 3] = got[:, 128:]

        def ranged(b):
            window = [azim[2 * b + j + tile_off] for j in range(4)]
            window[3] = window[3][:, :16]
            return jnp.dot(
                jnp.concatenate(window, axis=1), col_band, preferred_element_type=F32
            ).astype(BF)

        def put(t, value):
            lanes = pl.ds((t % HTILES) * 128, 128)
            first = t < HTILES

            @pl.when((core == 0) == first)
            def _():
                images[OWN0 + DATES * core + at, :, lanes] = value

            @pl.when((core == 0) != first)
            def _():
                other[i, :, lanes] = value

        for b in range(TILES // 2):
            got = ranged(b)
            put(2 * b, got[:, :128])
            put(2 * b + 1, got[:, 128:])

        @pl.when((i < MOVED) & far_ok)
        def _():
            far_copy(i, True).start()
            far_copy(i, False).start()

        pair_copy(i).start()

    def sums(x_at, others):
        count = len(others)

        @pl.loop(0, HTILES)
        def _(c):
            lanes = pl.ds(pl.multiple_of(c * 128, 128), 128)
            x = images[x_at, :, lanes]
            x0, x1 = x[:LINES], x[LINES:]

            def looked_lines(v):
                return (v[:LROWS] + v[LROWS : 2 * LROWS]) + (
                    v[2 * LROWS : 3 * LROWS] + v[3 * LROWS :]
                )

            lhs[pl.ds(0, LROWS), lanes] = looked_lines(x0 * x0 + x1 * x1)
            for n, y_at in enumerate(others):
                y = images[y_at, :, lanes]
                y0, y1 = y[:LINES], y[LINES:]
                row = LROWS * (1 + 2 * n)
                lhs[pl.ds(row, LROWS), lanes] = looked_lines(y0 * x0 + y1 * x1)
                lhs[pl.ds(row + LROWS, LROWS), lanes] = looked_lines(y1 * x0 - y0 * x1)

        total = jnp.dot(
            lhs[pl.ds(0, LROWS * (1 + 2 * count))], look[...], preferred_element_type=F32
        )
        here = total[:LROWS]
        power[x_at] = here
        results = []
        for n, y_at in enumerate(others):
            scale = 1.0 / jnp.sqrt(here * power[y_at] + EPSILON)
            row = LROWS * (1 + 2 * n)
            results.append((total[row : row + LROWS] * scale, total[row + LROWS : row + 2 * LROWS] * scale))
        return results

    def result_copy(u):
        return pltpu.make_async_remote_copy(
            src_ref=mine.at[u],
            dst_ref=theirs.at[u],
            send_sem=res_send.at[u],
            recv_sem=res_recv.at[u],
            device_id=(partner, s),
            device_id_type=MESH,
        )

    def later(u, first_lag, last_lag):
        x_at = OWN0 + u
        lag_list = list(range(first_lag, last_lag + 1))
        results = sums(x_at, [x_at - lag for lag in lag_list])
        for lag, (re_part, im_part) in zip(lag_list, results):
            mine[u - UFIRST, lag - MINLAG, 0] = re_part
            mine[u - UFIRST, lag - MINLAG, 1] = im_part
        result_copy(u - UFIRST).start()

    @pl.loop(0, DATES)
    def _(i):
        pair_copy(i).wait_recv()

    @pl.loop(0, MINLAG)
    def _(u):
        sums(OWN0 + u, [])

    for u in range(MINLAG, MAXLAG):
        later(u, MINLAG, u)

    @pl.loop(MAXLAG, 2 * DATES)
    def _(u):
        later(u, MINLAG, MAXLAG)

    def back_copy(i):
        return pltpu.make_async_remote_copy(
            src_ref=send_back.at[i],
            dst_ref=back.at[core, i],
            send_sem=back_send.at[i],
            recv_sem=back_recv.at[core, i],
            device_id=(2 * chip - 1, s),
            device_id_type=MESH,
        )

    for i in range(MOVED):
        @pl.when(has_next)
        def _():
            far_arrived(0, i).wait_recv()
            later(2 * DATES + i, max(MINLAG, i + 1), MAXLAG)

        @pl.when(has_prev)
        def _():
            far_arrived(1, i).wait_recv()
            results = sums(OWN0 - 1 - i, [OWN0 + u for u in range(MOVED, 2 * MOVED - i)])
            for n, (re_part, im_part) in enumerate(results):
                send_back[i, n, 0] = re_part
                send_back[i, n, 1] = -im_part
            back_copy(i).start()

    @pl.loop(0, 2 * DATES - UFIRST)
    def _(u):
        result_copy(u).wait_recv()

    @pl.when(has_next)
    def _():
        @pl.loop(2 * DATES - UFIRST, UCOUNT)
        def _(u):
            result_copy(u).wait_recv()

    def back_arrived(half, i):
        return pltpu.make_async_remote_copy(
            src_ref=send_back.at[i], dst_ref=back.at[half, i],
            send_sem=back_send.at[i], recv_sem=back_recv.at[half, i],
            device_id=(partner, s), device_id_type=MESH,
        )

    @pl.when(has_next & (core == 1))
    def _():
        for i in range(MOVED):
            back_arrived(0, i).wait_recv()
            back_arrived(1, i).wait_recv()

    @pl.loop(0, DATES)
    def _(j):
        t = DATES * core + j
        row = jnp.clip(2 * DATES - 1 - t, 0, MOVED - 1)
        for slot in range(4):
            lag = lags[j, slot]
            u = t + lag
            at = jnp.clip(u - UFIRST, 0, UCOUNT - 1)
            which = jnp.clip(lag - MINLAG, 0, LAGS - 1)
            far_at = jnp.clip(u - 2 * DATES - MOVED, 0, MOVED - 1)
            from_back = u >= 2 * DATES + MOVED
            for part in range(2):
                own, got = mine[at, which, part], theirs[at, which, part]
                left = jnp.where(core == 0, own, got)
                right = jnp.where(core == 0, got, own)
                left = jnp.where(from_back, back[0, row, far_at, part], left)
                right = jnp.where(from_back, back[1, row, far_at, part], right)
                value = jnp.concatenate([left, right], axis=1)
                out[j, slot, part] = jnp.where(lag > 0, value, 0.0)

    @pl.loop(0, DATES)
    def _(i):
        @pl.when(has_down)
        def _():
            edge_copy(i, 0).wait_send()

        @pl.when(has_up)
        def _():
            edge_copy(i, 1).wait_send()

        pair_copy(i).wait_send()

    @pl.when(far_ok)
    def _():
        @pl.loop(0, MOVED)
        def _(i):
            far_copy(i, True).wait_send()
            far_copy(i, False).wait_send()

    @pl.loop(0, 2 * DATES - UFIRST)
    def _(u):
        result_copy(u).wait_send()

    @pl.when(has_next)
    def _():
        @pl.loop(2 * DATES - UFIRST, UCOUNT)
        def _(u):
            result_copy(u).wait_send()

    @pl.when(has_prev)
    def _():
        @pl.loop(0, MOVED)
        def _(i):
            back_copy(i).wait_send()


def on_device(raw_slc, line_shift, line_phase, col_shift, col_phase, pair_lags):
    smem = pl.BlockSpec(memory_space=pltpu.SMEM)
    dma = pltpu.SemaphoreType.DMA
    part = (2, LROWS, LOOKS)
    return pl.pallas_call(
        kernel,
        out_shape=jax.ShapeDtypeStruct((DATES, 4, 2, LROWS, 2 * LOOKS), F32),
        in_specs=[pl.BlockSpec(memory_space=pl.ANY)] + [smem] * 6,
        out_specs=pl.BlockSpec(memory_space=pltpu.VMEM),
        scratch_shapes=[
            pltpu.VMEM((IMAGES, ROWS, HALF), BF),
            pltpu.VMEM((DATES, ROWS, HALF), BF),
            pltpu.VMEM((DATES, 2, EDGE, 2, COLS), BF),
            pltpu.VMEM((2, TILES, SRC, 2, 128), BF),
            pltpu.VMEM((TILES + 5, ROWS, 128), BF),
            pltpu.VMEM((LROWS * (1 + 2 * LAGS), HALF), BF),
            pltpu.VMEM((HALF, LOOKS), BF),
            pltpu.VMEM((IMAGES, LROWS, LOOKS), F32),
            pltpu.VMEM((UCOUNT, LAGS) + part, F32),
            pltpu.VMEM((UCOUNT, LAGS) + part, F32),
            pltpu.VMEM((2, MOVED, MOVED) + part, F32),
            pltpu.VMEM((MOVED, MOVED) + part, F32),
            dma((2,)),
            dma((DATES, 2)),
            dma((DATES, 2)),
            dma((DATES,)),
            dma((DATES,)),
            dma((MOVED, 2)),
            dma((2, MOVED)),
            dma((UCOUNT,)),
            dma((UCOUNT,)),
            dma((MOVED,)),
            dma((2, MOVED)),
        ],
        compiler_params=pltpu.CompilerParams(
            collective_id=0, has_side_effects=True, vmem_limit_bytes=56 * 1024 * 1024
        ),
        name="coherence_stack",
    )(raw_slc, line_shift, line_phase, col_shift, col_phase, pair_lags, jnp.asarray(sinc_table()))


def solution(mesh):
    return jax.shard_map(
        on_device,
        mesh=mesh,
        in_specs=(
            P("date", "strip", None, None),
            P("date"),
            P("date"),
            P("date"),
            P("date"),
            P("date", None),
        ),
        out_specs=P("date", None, None, "strip", None),
        check_vma=False,
    )
```

time: 652 us -> 88.4 us (0.14)
  the two profiles are of different devices: /device:TPU:36 before, /device:TPU:31 now
where the time goes in v1:
time: 88.4 us; the launch traced here: 88.2 us
  Pallas kernels  84.5 us (96%)
  local copies, waits for them, and re-layouts  3.65 us (4%)
    pallas_call x1, Pallas kernels, on_device(): pl.pallas_call(kernel, out_shape=jax.ShapeDtypeStruct((DATES, 4, 2, LROWS...  84.5 us
    unnamed x2, local copies, waits for them, and re-layouts  3.65 us

profile of v1, /device:TPU:31, one launch (start us, length us, event | category | flops | bytes accessed | tf_op | source)
XLA Modules:
  0.0 88.2 jit_solution(11829662776653211906)
XLA Ops:
  0.0 1.3 %copy.8.lags = s32[8,4]{1,0:T(8,128)} copy(s32[8,4]{0,1:T(4,128)} %param.12) | data formatting | bytes 256 | tf_op args[5]
  1.3 84.5 %coherence_stack.1 = f32[8,4,2,16,192]{4,3,2,1,0:T(8,128)} custom-call(bf16[8,64,2,3840]{3,2,1,0:T(2,128)(2,1)} %raw.1, s32[8]{0:T(128)} %line_shift.1, s32[8]{0:T(128)} %line_phase.1, s32[8]{0:T(128)} %col_shift.1, s32[8]{0:T(128)} %col_phase.1, s32[8,4]{1,0:T(8,128)} %copy.8.lags, f32[128]{0:T(128)} %constant.2.clone.table), custom_call_target="tpu_custom_call" | custom-call | tf_op jit(solution)/shard_map/coherence_stack/pallas_call | solution.py:453
  85.9 2.3 %copy.10 = f32[8,4,2,16,192]{4,3,2,1,0:T(8,128)} copy(f32[8,4,2,16,192]{4,3,2,1,0:T(8,128)} %coherence_stack.1) | data formatting | bytes 1572864

commit v2 on v1

--- a/solution.py
+++ b/solution.py
@@ -32,6 +32,9 @@
 OWN0 = MOVED
 NEXT0 = OWN0 + 2 * DATES
 IMAGES = NEXT0 + MOVED
+RELAYED = (1, 2)
+RELAYS = ((7, 14, 8), (7, 15, 9), (8, 0, 6), (8, 1, 7))
+OTHER0 = IMAGES
 UFIRST = MINLAG
 UCOUNT = 2 * DATES + MOVED - UFIRST
 
@@ -51,9 +54,9 @@
 def kernel(
     raw, line_shift, line_phase, col_shift, col_phase, lags, table,
     out,
-    images, other, halo, src, azim, lhs, look, power, mine, theirs, back, send_back,
+    images, relay, halo, src, azim, lhs, look, power, mine, theirs, back, send_back,
     load_sem, halo_send, halo_recv, pair_send, pair_recv, far_send, far_recv,
-    res_send, res_recv, back_send, back_recv,
+    res_send, res_recv, back_send, back_recv, relay_send, relay_recv,
 ):
     d, s = lax.axis_index("date"), lax.axis_index("strip")
     n_date, n_strip = lax.axis_size("date"), lax.axis_size("strip")
@@ -67,6 +70,10 @@
     far_ok = jnp.where(core == 0, has_prev, has_next)
     far_chip = jnp.where(core == 0, chip - 1, chip + 1)
 
+    crossing = (d == 7) | (d == 8)
+    relaying = (d < 2) | (d >= n_date - 2)
+    across = (s + n_strip // 2) % n_strip
+
     def place(i):
         return jnp.where(core == 0, i, DATES - 1 - i)
 
@@ -114,6 +121,14 @@
         def _():
             pl.semaphore_signal(barrier, inc=1, device_id=(d, s + step), device_id_type=MESH)
 
+    for a, b in sorted({(min(p), max(p)) for x, y, z in RELAYS for p in ((x, y), (y, z))}):
+        for here, there in ((a, b), (b, a)):
+            peers = peers + (d == here).astype(jnp.int32)
+
+            @pl.when(d == here)
+            def _():
+                pl.semaphore_signal(barrier, inc=1, device_id=(there, across), device_id_type=MESH)
+
     pl.semaphore_wait(barrier, peers)
 
     def edge_copy(i, side):
@@ -126,8 +141,7 @@
             device_id_type=MESH,
         )
 
-    @pl.loop(0, DATES)
-    def _(i):
+    def edge_start(i):
         @pl.when(has_down)
         def _():
             edge_copy(i, 0).start()
@@ -135,6 +149,8 @@
         @pl.when(has_up)
         def _():
             edge_copy(i, 1).start()
+
+    edge_start(0)
 
     @pl.when(jnp.logical_not(has_up))
     def _():
@@ -165,17 +181,55 @@
         def _():
             edge_copy(i, 1).wait_recv()
 
-    def far_copy(i, half_own):
-        at = jnp.where(core == 0, NEXT0 + i, OWN0 - 1 - i)
-        target = 2 * far_chip + (core if half_own else 1 - core)
-        return pltpu.make_async_remote_copy(
-            src_ref=images.at[OWN0 + DATES * core + place(i)] if half_own else other.at[i],
-            dst_ref=images.at[at],
-            send_sem=far_send.at[i, 1 if half_own else 0],
+    def half_place(i, half):
+        return jnp.where(core == half, OWN0 + DATES * core + place(i), OTHER0 + i)
+
+    def far_copy(i, half):
+        return pltpu.make_async_remote_copy(
+            src_ref=images.at[half_place(i, half)],
+            dst_ref=images.at[jnp.where(core == 0, NEXT0 + i, OWN0 - 1 - i)],
+            send_sem=far_send.at[i, half],
             recv_sem=far_recv.at[core, i],
-            device_id=(target, s),
-            device_id_type=MESH,
-        )
+            device_id=(2 * far_chip + half, s),
+            device_id_type=MESH,
+        )
+
+    def relay_in(i, half):
+        return pltpu.make_async_remote_copy(
+            src_ref=images.at[half_place(i, half)],
+            dst_ref=relay.at[i - RELAYED[0]],
+            send_sem=far_send.at[i, half],
+            recv_sem=relay_recv.at[i - RELAYED[0]],
+            device_id=(jnp.where(d == 7, n_date - 2, 0) + half, across),
+            device_id_type=MESH,
+        )
+
+    def relay_out(i):
+        return pltpu.make_async_remote_copy(
+            src_ref=relay.at[i - RELAYED[0]],
+            dst_ref=images.at[jnp.where(d < 2, NEXT0 + i, OWN0 - 1 - i)],
+            send_sem=relay_send.at[i - RELAYED[0]],
+            recv_sem=far_recv.at[jnp.where(d < 2, 0, 1), i],
+            device_id=(jnp.where(d < 2, d + 6, d - 6), across),
+            device_id_type=MESH,
+        )
+
+    def pass_on(i):
+        @pl.when(relaying)
+        def _():
+            relay_in(i, 0).wait_recv()
+            relay_out(i).start()
+
+    def far_start(i, half):
+        relayed = crossing & (i >= RELAYED[0]) & (i <= RELAYED[-1])
+
+        @pl.when((i < MOVED) & far_ok & jnp.logical_not(relayed))
+        def _():
+            far_copy(i, half).start()
+
+        @pl.when(relayed)
+        def _():
+            relay_in(i, half).start()
 
     def far_arrived(side, i):
         at = NEXT0 + i if side == 0 else OWN0 - 1 - i
@@ -187,7 +241,7 @@
 
     def pair_copy(i):
         return pltpu.make_async_remote_copy(
-            src_ref=other.at[i],
+            src_ref=images.at[OTHER0 + i],
             dst_ref=images.at[OWN0 + DATES * core + place(i)],
             send_sem=pair_send.at[i],
             recv_sem=pair_recv.at[i],
@@ -204,6 +258,7 @@
         jnp.int32, (256, 256), 1
     )
 
+    edge_start(1)
     edge_wait(0)
     start_edges(0, 0)
 
@@ -218,8 +273,10 @@
         @pl.when(i < DATES - 1)
         def _():
             start_lines(i + 1, 1 - slot)
-            edge_wait(i + 1)
-            start_edges(i + 1, 1 - slot)
+
+        @pl.when(i < DATES - 2)
+        def _():
+            edge_start(i + 2)
 
         line_off, line_ph = line_shift[at], line_phase[at]
         col_off, col_ph = col_shift[at] - (TAPS // 2 - 1) + 256, col_phase[at]
@@ -243,6 +300,11 @@
             azim[2 * b + 2] = got[:, :128]
             azim[2 * b + 3] = got[:, 128:]
 
+        @pl.when(i < DATES - 1)
+        def _():
+            edge_wait(i + 1)
+            start_edges(i + 1, 1 - slot)
+
         def ranged(b):
             window = [azim[2 * b + j + tile_off] for j in range(4)]
             window[3] = window[3][:, :16]
@@ -250,28 +312,18 @@
                 jnp.concatenate(window, axis=1), col_band, preferred_element_type=F32
             ).astype(BF)
 
+        half_at = [half_place(i, half) for half in range(2)]
+
         def put(t, value):
-            lanes = pl.ds((t % HTILES) * 128, 128)
-            first = t < HTILES
-
-            @pl.when((core == 0) == first)
-            def _():
-                images[OWN0 + DATES * core + at, :, lanes] = value
-
-            @pl.when((core == 0) != first)
-            def _():
-                other[i, :, lanes] = value
+            images[half_at[t // HTILES], :, pl.ds((t % HTILES) * 128, 128)] = value
 
         for b in range(TILES // 2):
             got = ranged(b)
             put(2 * b, got[:, :128])
             put(2 * b + 1, got[:, 128:])
-
-        @pl.when((i < MOVED) & far_ok)
-        def _():
-            far_copy(i, True).start()
-            far_copy(i, False).start()
-
+            if 2 * b + 1 == HTILES:
+                far_start(i, 0)
+        far_start(i, 1)
         pair_copy(i).start()
 
     def sums(x_at, others):
@@ -331,6 +383,8 @@
     def _(i):
         pair_copy(i).wait_recv()
 
+    pass_on(RELAYED[0])
+
     @pl.loop(0, MINLAG)
     def _(u):
         sums(OWN0 + u, [])
@@ -338,14 +392,17 @@
     for u in range(MINLAG, MAXLAG):
         later(u, MINLAG, u)
 
+    for i in RELAYED[1:]:
+        pass_on(i)
+
     @pl.loop(MAXLAG, 2 * DATES)
     def _(u):
         later(u, MINLAG, MAXLAG)
 
     def back_copy(i):
         return pltpu.make_async_remote_copy(
-            src_ref=send_back.at[i],
-            dst_ref=back.at[core, i],
+            src_ref=send_back.at[i, pl.ds(0, MOVED - i)],
+            dst_ref=back.at[core, i, pl.ds(0, MOVED - i)],
             send_sem=back_send.at[i],
             recv_sem=back_recv.at[core, i],
             device_id=(2 * chip - 1, s),
@@ -353,19 +410,19 @@
         )
 
     for i in range(MOVED):
-        @pl.when(has_next)
-        def _():
-            far_arrived(0, i).wait_recv()
-            later(2 * DATES + i, max(MINLAG, i + 1), MAXLAG)
-
         @pl.when(has_prev)
         def _():
             far_arrived(1, i).wait_recv()
             results = sums(OWN0 - 1 - i, [OWN0 + u for u in range(MOVED, 2 * MOVED - i)])
             for n, (re_part, im_part) in enumerate(results):
-                send_back[i, n, 0] = re_part
-                send_back[i, n, 1] = -im_part
+                send_back[i, n, 0] = re_part.astype(BF)
+                send_back[i, n, 1] = (-im_part).astype(BF)
             back_copy(i).start()
+
+        @pl.when(has_next)
+        def _():
+            far_arrived(0, i).wait_recv()
+            later(2 * DATES + i, max(MINLAG, i + 1), MAXLAG)
 
     @pl.loop(0, 2 * DATES - UFIRST)
     def _(u):
@@ -379,7 +436,8 @@
 
     def back_arrived(half, i):
         return pltpu.make_async_remote_copy(
-            src_ref=send_back.at[i], dst_ref=back.at[half, i],
+            src_ref=send_back.at[i, pl.ds(0, MOVED - i)],
+            dst_ref=back.at[half, i, pl.ds(0, MOVED - i)],
             send_sem=back_send.at[i], recv_sem=back_recv.at[half, i],
             device_id=(partner, s), device_id_type=MESH,
         )
@@ -395,7 +453,7 @@
         t = DATES * core + j
         row = jnp.clip(2 * DATES - 1 - t, 0, MOVED - 1)
         for slot in range(4):
-            lag = lags[j, slot]
+            lag = lags[slot, j]
             u = t + lag
             at = jnp.clip(u - UFIRST, 0, UCOUNT - 1)
             which = jnp.clip(lag - MINLAG, 0, LAGS - 1)
@@ -405,8 +463,8 @@
                 own, got = mine[at, which, part], theirs[at, which, part]
                 left = jnp.where(core == 0, own, got)
                 right = jnp.where(core == 0, got, own)
-                left = jnp.where(from_back, back[0, row, far_at, part], left)
-                right = jnp.where(from_back, back[1, row, far_at, part], right)
+                left = jnp.where(from_back, back[0, row, far_at, part].astype(F32), left)
+                right = jnp.where(from_back, back[1, row, far_at, part].astype(F32), right)
                 value = jnp.concatenate([left, right], axis=1)
                 out[j, slot, part] = jnp.where(lag > 0, value, 0.0)
 
@@ -426,8 +484,8 @@
     def _():
         @pl.loop(0, MOVED)
         def _(i):
-            far_copy(i, True).wait_send()
-            far_copy(i, False).wait_send()
+            far_copy(i, 0).wait_send()
+            far_copy(i, 1).wait_send()
 
     @pl.loop(0, 2 * DATES - UFIRST)
     def _(u):
@@ -441,9 +499,13 @@
 
     @pl.when(has_prev)
     def _():
-        @pl.loop(0, MOVED)
-        def _(i):
+        for i in range(MOVED):
             back_copy(i).wait_send()
+
+    @pl.when(relaying)
+    def _():
+        for i in RELAYED:
+            relay_out(i).wait_send()
 
 
 def on_device(raw_slc, line_shift, line_phase, col_shift, col_phase, pair_lags):
@@ -456,8 +518,8 @@
         in_specs=[pl.BlockSpec(memory_space=pl.ANY)] + [smem] * 6,
         out_specs=pl.BlockSpec(memory_space=pltpu.VMEM),
         scratch_shapes=[
-            pltpu.VMEM((IMAGES, ROWS, HALF), BF),
-            pltpu.VMEM((DATES, ROWS, HALF), BF),
+            pltpu.VMEM((IMAGES + DATES, ROWS, HALF), BF),
+            pltpu.VMEM((len(RELAYED), ROWS, HALF), BF),
             pltpu.VMEM((DATES, 2, EDGE, 2, COLS), BF),
             pltpu.VMEM((2, TILES, SRC, 2, 128), BF),
             pltpu.VMEM((TILES + 5, ROWS, 128), BF),
@@ -466,8 +528,8 @@
             pltpu.VMEM((IMAGES, LROWS, LOOKS), F32),
             pltpu.VMEM((UCOUNT, LAGS) + part, F32),
             pltpu.VMEM((UCOUNT, LAGS) + part, F32),
-            pltpu.VMEM((2, MOVED, MOVED) + part, F32),
-            pltpu.VMEM((MOVED, MOVED) + part, F32),
+            pltpu.VMEM((2, MOVED, MOVED) + part, BF),
+            pltpu.VMEM((MOVED, MOVED) + part, BF),
             dma((2,)),
             dma((DATES, 2)),
             dma((DATES, 2)),
@@ -479,12 +541,14 @@
             dma((UCOUNT,)),
             dma((MOVED,)),
             dma((2, MOVED)),
+            dma((len(RELAYED),)),
+            dma((len(RELAYED),)),
         ],
         compiler_params=pltpu.CompilerParams(
             collective_id=0, has_side_effects=True, vmem_limit_bytes=56 * 1024 * 1024
         ),
         name="coherence_stack",
-    )(raw_slc, line_shift, line_phase, col_shift, col_phase, pair_lags, jnp.asarray(sinc_table()))
+    )(raw_slc, line_shift, line_phase, col_shift, col_phase, pair_lags.T, jnp.asarray(sinc_table()))
 
 
 def solution(mesh):

time: 88.4 us -> 77.3 us (0.87)
  the two profiles are of different devices: /device:TPU:31 before, /device:TPU:36 now
where the time goes in v2:
time: 77.3 us; the launch traced here: 77.2 us
  Pallas kernels  74.9 us (97%)
  local copies, waits for them, and re-layouts  2.31 us (3%)
    pallas_call x1, Pallas kernels, on_device(): pl.pallas_call(kernel, out_shape=jax.ShapeDtypeStruct((DATES, 4, 2, LROWS...  74.9 us
    unnamed x1, local copies, waits for them, and re-layouts  2.31 us

profile of v2, /device:TPU:36, one launch (start us, length us, event | category | flops | bytes accessed | tf_op | source)
XLA Modules:
  0.0 77.2 jit_solution(15753889334117327250)
XLA Ops:
  0.0 74.9 %coherence_stack.1 = f32[8,4,2,16,192]{4,3,2,1,0:T(8,128)} custom-call(bf16[8,64,2,3840]{3,2,1,0:T(2,128)(2,1)} %raw.1, s32[8]{0:T(128)} %line_shift.1, s32[8]{0:T(128)} %line_phase.1, s32[8]{0:T(128)} %col_shift.1, s32[8]{0:T(128)} %col_phase.1, s32[4,8]{1,0:T(4,128)} %bitcast.1, f32[128]{0:T(128)} %constant.2.clone.table), custom_call_target="tpu_custom_call" | custom-call | tf_op jit(solution)/shard_map/coherence_stack/pallas_call | solution.py:515
  74.9 2.3 %copy.9 = f32[8,4,2,16,192]{4,3,2,1,0:T(8,128)} copy(f32[8,4,2,16,192]{4,3,2,1,0:T(8,128)} %coherence_stack.1) | data formatting | bytes 1572864

commit v3 on v2

--- a/solution.py
+++ b/solution.py
@@ -32,8 +32,10 @@
 OWN0 = MOVED
 NEXT0 = OWN0 + 2 * DATES
 IMAGES = NEXT0 + MOVED
-RELAYED = (1, 2)
+RELAYED = (0, 1)
 RELAYS = ((7, 14, 8), (7, 15, 9), (8, 0, 6), (8, 1, 7))
+AHEAD = 4
+PASS_AT = 8
 OTHER0 = IMAGES
 UFIRST = MINLAG
 UCOUNT = 2 * DATES + MOVED - UFIRST
@@ -54,9 +56,10 @@
 def kernel(
     raw, line_shift, line_phase, col_shift, col_phase, lags, table,
     out,
-    images, relay, halo, src, azim, lhs, look, power, mine, theirs, back, send_back,
+    images, relay, halo, far_raw, far_shift, far_phase, far_col_shift, far_col_phase, shifts,
+    src, azim, lhs, look, power, mine, theirs, back, send_back,
     load_sem, halo_send, halo_recv, pair_send, pair_recv, far_send, far_recv,
-    res_send, res_recv, back_send, back_recv, relay_send, relay_recv,
+    res_send, res_recv, back_send, back_recv, relay_send, relay_recv, raw_send, raw_recv,
 ):
     d, s = lax.axis_index("date"), lax.axis_index("strip")
     n_date, n_strip = lax.axis_size("date"), lax.axis_size("strip")
@@ -77,9 +80,30 @@
     def place(i):
         return jnp.where(core == 0, i, DATES - 1 - i)
 
-    def load_tile(i, slot, c):
+    far_device = jnp.where(core == 0, d - 1, d + 1)
+    far_image = jnp.where(core == 0, OWN0 - 1, NEXT0)
+    has_raw = far_ok & jnp.logical_not(crossing)
+    partner_raw = jnp.where(core == 0, has_next & (chip != 3), has_prev & (chip != 4))
+
+    def raw_copies():
+        pairs = (
+            (raw.at[place(0)], far_raw),
+            (line_shift, far_shift),
+            (line_phase, far_phase),
+            (col_shift, far_col_shift),
+            (col_phase, far_col_phase),
+        )
+        return [
+            pltpu.make_async_remote_copy(
+                src_ref=a, dst_ref=b, send_sem=raw_send.at[n], recv_sem=raw_recv.at[n],
+                device_id=(far_device, s), device_id_type=MESH,
+            )
+            for n, (a, b) in enumerate(pairs)
+        ]
+
+    def load_tile(lines, slot, c):
         return pltpu.make_async_copy(
-            raw.at[place(i), :, :, pl.ds(pl.multiple_of(c * 128, 128), 128)],
+            lines.at[:, :, pl.ds(pl.multiple_of(c * 128, 128), 128)],
             src.at[slot, c, pl.ds(EDGE, LINES)],
             load_sem.at[slot],
         )
@@ -91,10 +115,10 @@
             load_sem.at[slot],
         )
 
-    def start_lines(i, slot):
+    def start_lines(lines, slot):
         @pl.loop(0, TILES)
         def _(c):
-            load_tile(i, slot, c).start()
+            load_tile(lines, slot, c).start()
 
     def start_edges(i, slot):
         @pl.loop(0, TILES)
@@ -102,7 +126,7 @@
             load_edges(i, slot, c, 0).start()
             load_edges(i, slot, c, 1).start()
 
-    start_lines(0, 0)
+    start_lines(raw.at[place(0)], 0)
 
     barrier = pltpu.get_barrier_semaphore()
     peers = 0
@@ -131,9 +155,11 @@
 
     pl.semaphore_wait(barrier, peers)
 
-    def edge_copy(i, side):
-        return pltpu.make_async_remote_copy(
-            src_ref=raw.at[place(i), pl.ds((1 - side) * (LINES - EDGE), EDGE)],
+    def edge_copy(lines, i, side):
+        return pltpu.make_async_remote_copy(
+            src_ref=halo.at[i, side] if lines is None else lines.at[
+                pl.ds((1 - side) * (LINES - EDGE), EDGE)
+            ],
             dst_ref=halo.at[i, side],
             send_sem=halo_send.at[i, side],
             recv_sem=halo_recv.at[i, side],
@@ -141,26 +167,31 @@
             device_id_type=MESH,
         )
 
-    def edge_start(i):
+    def edge_start(lines, i):
         @pl.when(has_down)
         def _():
-            edge_copy(i, 0).start()
+            edge_copy(lines, i, 0).start()
 
         @pl.when(has_up)
         def _():
-            edge_copy(i, 1).start()
-
-    edge_start(0)
+            edge_copy(lines, i, 1).start()
+
+    edge_start(raw.at[place(0)], 0)
+
+    @pl.when(has_raw)
+    def _():
+        for copy in raw_copies():
+            copy.start()
 
     @pl.when(jnp.logical_not(has_up))
     def _():
-        @pl.loop(0, DATES)
+        @pl.loop(0, DATES + 1)
         def _(i):
             halo[i, 0] = jnp.zeros((EDGE, 2, COLS), BF)
 
     @pl.when(jnp.logical_not(has_down))
     def _():
-        @pl.loop(0, DATES)
+        @pl.loop(0, DATES + 1)
         def _(i):
             halo[i, 1] = jnp.zeros((EDGE, 2, COLS), BF)
 
@@ -175,14 +206,17 @@
     def edge_wait(i):
         @pl.when(has_up)
         def _():
-            edge_copy(i, 0).wait_recv()
+            edge_copy(None, i, 0).wait_recv()
 
         @pl.when(has_down)
         def _():
-            edge_copy(i, 1).wait_recv()
+            edge_copy(None, i, 1).wait_recv()
+
+    def own_place(i):
+        return jnp.where(i < DATES, OWN0 + DATES * core + place(i), far_image)
 
     def half_place(i, half):
-        return jnp.where(core == half, OWN0 + DATES * core + place(i), OTHER0 + i)
+        return jnp.where(core == half, own_place(i), OTHER0 + i)
 
     def far_copy(i, half):
         return pltpu.make_async_remote_copy(
@@ -223,7 +257,9 @@
     def far_start(i, half):
         relayed = crossing & (i >= RELAYED[0]) & (i <= RELAYED[-1])
 
-        @pl.when((i < MOVED) & far_ok & jnp.logical_not(relayed))
+        direct = far_ok & (i < MOVED) & ((i > 0) | crossing) & jnp.logical_not(relayed)
+
+        @pl.when(direct)
         def _():
             far_copy(i, half).start()
 
@@ -242,7 +278,7 @@
     def pair_copy(i):
         return pltpu.make_async_remote_copy(
             src_ref=images.at[OTHER0 + i],
-            dst_ref=images.at[OWN0 + DATES * core + place(i)],
+            dst_ref=images.at[own_place(i)],
             send_sem=pair_send.at[i],
             recv_sem=pair_recv.at[i],
             device_id=(partner, s),
@@ -258,28 +294,51 @@
         jnp.int32, (256, 256), 1
     )
 
-    edge_start(1)
+    for n in range(1, AHEAD):
+        edge_start(raw.at[place(n)], n)
     edge_wait(0)
     start_edges(0, 0)
 
-    @pl.loop(0, DATES)
+    count = DATES + has_raw.astype(jnp.int32)
+
+    @pl.loop(0, count)
     def _(i):
         slot = i % 2
-        at = place(i)
+        at = jnp.where(i < DATES, place(i), jnp.where(core == 0, DATES - 1, 0))
         pltpu.make_async_copy(
             src.at[slot], src.at[slot], load_sem.at[slot]
         ).wait()
 
         @pl.when(i < DATES - 1)
         def _():
-            start_lines(i + 1, 1 - slot)
-
-        @pl.when(i < DATES - 2)
-        def _():
-            edge_start(i + 2)
-
-        line_off, line_ph = line_shift[at], line_phase[at]
-        col_off, col_ph = col_shift[at] - (TAPS // 2 - 1) + 256, col_phase[at]
+            start_lines(raw.at[place(i + 1)], 1 - slot)
+
+        @pl.when((i == DATES - 1) & has_raw)
+        def _():
+            start_lines(far_raw, 1 - slot)
+
+        @pl.when(i < DATES - AHEAD)
+        def _():
+            edge_start(raw.at[place(i + AHEAD)], i + AHEAD)
+
+        @pl.when((i == DATES - 2) & has_raw)
+        def _():
+            for copy in raw_copies():
+                copy.wait_recv()
+            edge_start(far_raw, DATES)
+
+        @pl.when(i < DATES)
+        def _():
+            for n, of_date in enumerate((line_shift, line_phase, col_shift, col_phase)):
+                shifts[n] = of_date[at]
+
+        @pl.when(i >= DATES)
+        def _():
+            for n, of_date in enumerate((far_shift, far_phase, far_col_shift, far_col_phase)):
+                shifts[n] = of_date[at]
+
+        line_off, line_ph, col_off, col_ph = (shifts[n] for n in range(4))
+        col_off = col_off - (TAPS // 2 - 1) + 256
         tile_off, rest = col_off // 128, col_off % 128
         line_band = jnp.zeros((ROWS, 2 * SRC), F32)
         band0 = jnp.zeros((256, 256), F32)
@@ -300,7 +359,7 @@
             azim[2 * b + 2] = got[:, :128]
             azim[2 * b + 3] = got[:, 128:]
 
-        @pl.when(i < DATES - 1)
+        @pl.when(i < count - 1)
         def _():
             edge_wait(i + 1)
             start_edges(i + 1, 1 - slot)
@@ -379,11 +438,11 @@
             mine[u - UFIRST, lag - MINLAG, 1] = im_part
         result_copy(u - UFIRST).start()
 
-    @pl.loop(0, DATES)
+    pass_on(RELAYED[0])
+
+    @pl.loop(0, DATES + partner_raw.astype(jnp.int32))
     def _(i):
         pair_copy(i).wait_recv()
-
-    pass_on(RELAYED[0])
 
     @pl.loop(0, MINLAG)
     def _(u):
@@ -391,9 +450,8 @@
 
     for u in range(MINLAG, MAXLAG):
         later(u, MINLAG, u)
-
-    for i in RELAYED[1:]:
-        pass_on(i)
+        if u == PASS_AT:
+            pass_on(RELAYED[1])
 
     @pl.loop(MAXLAG, 2 * DATES)
     def _(u):
@@ -412,7 +470,10 @@
     for i in range(MOVED):
         @pl.when(has_prev)
         def _():
-            far_arrived(1, i).wait_recv()
+            @pl.when((i > 0) | (chip == 4))
+            def _():
+                far_arrived(1, i).wait_recv()
+
             results = sums(OWN0 - 1 - i, [OWN0 + u for u in range(MOVED, 2 * MOVED - i)])
             for n, (re_part, im_part) in enumerate(results):
                 send_back[i, n, 0] = re_part.astype(BF)
@@ -421,7 +482,10 @@
 
         @pl.when(has_next)
         def _():
-            far_arrived(0, i).wait_recv()
+            @pl.when((i > 0) | (chip == 3))
+            def _():
+                far_arrived(0, i).wait_recv()
+
             later(2 * DATES + i, max(MINLAG, i + 1), MAXLAG)
 
     @pl.loop(0, 2 * DATES - UFIRST)
@@ -468,21 +532,26 @@
                 value = jnp.concatenate([left, right], axis=1)
                 out[j, slot, part] = jnp.where(lag > 0, value, 0.0)
 
-    @pl.loop(0, DATES)
+    @pl.loop(0, count)
     def _(i):
         @pl.when(has_down)
         def _():
-            edge_copy(i, 0).wait_send()
+            edge_copy(None, i, 0).wait_send()
 
         @pl.when(has_up)
         def _():
-            edge_copy(i, 1).wait_send()
+            edge_copy(None, i, 1).wait_send()
 
         pair_copy(i).wait_send()
 
+    @pl.when(has_raw)
+    def _():
+        for copy in raw_copies():
+            copy.wait_send()
+
     @pl.when(far_ok)
     def _():
-        @pl.loop(0, MOVED)
+        @pl.loop(jnp.where(crossing, 0, 1), MOVED)
         def _(i):
             far_copy(i, 0).wait_send()
             far_copy(i, 1).wait_send()
@@ -518,9 +587,15 @@
         in_specs=[pl.BlockSpec(memory_space=pl.ANY)] + [smem] * 6,
         out_specs=pl.BlockSpec(memory_space=pltpu.VMEM),
         scratch_shapes=[
-            pltpu.VMEM((IMAGES + DATES, ROWS, HALF), BF),
+            pltpu.VMEM((IMAGES + DATES + 1, ROWS, HALF), BF),
             pltpu.VMEM((len(RELAYED), ROWS, HALF), BF),
-            pltpu.VMEM((DATES, 2, EDGE, 2, COLS), BF),
+            pltpu.VMEM((DATES + 1, 2, EDGE, 2, COLS), BF),
+            pltpu.VMEM((LINES, 2, COLS), BF),
+            pltpu.SMEM((DATES,), jnp.int32),
+            pltpu.SMEM((DATES,), jnp.int32),
+            pltpu.SMEM((DATES,), jnp.int32),
+            pltpu.SMEM((DATES,), jnp.int32),
+            pltpu.SMEM((4,), jnp.int32),
             pltpu.VMEM((2, TILES, SRC, 2, 128), BF),
             pltpu.VMEM((TILES + 5, ROWS, 128), BF),
             pltpu.VMEM((LROWS * (1 + 2 * LAGS), HALF), BF),
@@ -531,10 +606,10 @@
             pltpu.VMEM((2, MOVED, MOVED) + part, BF),
             pltpu.VMEM((MOVED, MOVED) + part, BF),
             dma((2,)),
-            dma((DATES, 2)),
-            dma((DATES, 2)),
-            dma((DATES,)),
-            dma((DATES,)),
+            dma((DATES + 1, 2)),
+            dma((DATES + 1, 2)),
+            dma((DATES + 1,)),
+            dma((DATES + 1,)),
             dma((MOVED, 2)),
             dma((2, MOVED)),
             dma((UCOUNT,)),
@@ -543,6 +618,8 @@
             dma((2, MOVED)),
             dma((len(RELAYED),)),
             dma((len(RELAYED),)),
+            dma((5,)),
+            dma((5,)),
         ],
         compiler_params=pltpu.CompilerParams(
             collective_id=0, has_side_effects=True, vmem_limit_bytes=56 * 1024 * 1024

time: 77.3 us -> 72.9 us (0.943)
  the two profiles are of different devices: /device:TPU:36 before, /device:TPU:7 now
where the time goes in v3:
time: 72.9 us; the launch traced here: 72.7 us
  Pallas kernels  70.4 us (97%)
  local copies, waits for them, and re-layouts  2.31 us (3%)
    pallas_call x1, Pallas kernels, on_device(): pl.pallas_call(kernel, out_shape=jax.ShapeDtypeStruct((DATES, 4, 2, LROWS...  70.4 us
    unnamed x1, local copies, waits for them, and re-layouts  2.31 us

profile of v3, /device:TPU:7, one launch (start us, length us, event | category | flops | bytes accessed | tf_op | source)
XLA Modules:
  0.0 72.7 jit_solution(14503284313196791525)
XLA Ops:
  0.0 70.4 %coherence_stack.1 = f32[8,4,2,16,192]{4,3,2,1,0:T(8,128)} custom-call(bf16[8,64,2,3840]{3,2,1,0:T(2,128)(2,1)} %raw.1, s32[8]{0:T(128)} %line_shift.1, s32[8]{0:T(128)} %line_phase.1, s32[8]{0:T(128)} %col_shift.1, s32[8]{0:T(128)} %col_phase.1, s32[4,8]{1,0:T(4,128)} %bitcast.1, f32[128]{0:T(128)} %constant.2.clone.table), custom_call_target="tpu_custom_call" | custom-call | tf_op jit(solution)/shard_map/coherence_stack/pallas_call | solution.py:584
  70.4 2.3 %copy.9 = f32[8,4,2,16,192]{4,3,2,1,0:T(8,128)} copy(f32[8,4,2,16,192]{4,3,2,1,0:T(8,128)} %coherence_stack.1) | data formatting | bytes 1572864

commit v4 on v3

--- a/solution.py
+++ b/solution.py
@@ -35,7 +35,8 @@
 RELAYED = (0, 1)
 RELAYS = ((7, 14, 8), (7, 15, 9), (8, 0, 6), (8, 1, 7))
 AHEAD = 4
-PASS_AT = 8
+PASS_AT = 6
+CROSSED_ORDER = (2, 3, 0, 4, 1)
 OTHER0 = IMAGES
 UFIRST = MINLAG
 UCOUNT = 2 * DATES + MOVED - UFIRST
@@ -440,15 +441,21 @@
 
     pass_on(RELAYED[0])
 
-    @pl.loop(0, DATES + partner_raw.astype(jnp.int32))
-    def _(i):
-        pair_copy(i).wait_recv()
+    def pairs_arrived(first, end):
+        @pl.loop(first, end)
+        def _(i):
+            pair_copy(i).wait_recv()
+
+    pairs_arrived(0, MINLAG)
 
     @pl.loop(0, MINLAG)
     def _(u):
         sums(OWN0 + u, [])
 
+    pairs_arrived(MINLAG, DATES - 1)
     for u in range(MINLAG, MAXLAG):
+        if u == DATES - 1:
+            pairs_arrived(DATES - 1, DATES)
         later(u, MINLAG, u)
         if u == PASS_AT:
             pass_on(RELAYED[1])
@@ -456,6 +463,10 @@
     @pl.loop(MAXLAG, 2 * DATES)
     def _(u):
         later(u, MINLAG, MAXLAG)
+
+    @pl.when(partner_raw)
+    def _():
+        pair_copy(DATES).wait_recv()
 
     def back_copy(i):
         return pltpu.make_async_remote_copy(
@@ -467,26 +478,25 @@
             device_id_type=MESH,
         )
 
-    for i in range(MOVED):
-        @pl.when(has_prev)
-        def _():
-            @pl.when((i > 0) | (chip == 4))
-            def _():
-                far_arrived(1, i).wait_recv()
-
-            results = sums(OWN0 - 1 - i, [OWN0 + u for u in range(MOVED, 2 * MOVED - i)])
-            for n, (re_part, im_part) in enumerate(results):
-                send_back[i, n, 0] = re_part.astype(BF)
-                send_back[i, n, 1] = (-im_part).astype(BF)
-            back_copy(i).start()
-
-        @pl.when(has_next)
-        def _():
-            @pl.when((i > 0) | (chip == 3))
-            def _():
-                far_arrived(0, i).wait_recv()
-
-            later(2 * DATES + i, max(MINLAG, i + 1), MAXLAG)
+    def from_next(i, sent):
+        if sent:
+            far_arrived(0, i).wait_recv()
+        later(2 * DATES + i, max(MINLAG, i + 1), MAXLAG)
+
+    def from_prev(i, sent):
+        if sent:
+            far_arrived(1, i).wait_recv()
+        results = sums(OWN0 - 1 - i, [OWN0 + u for u in range(MOVED, 2 * MOVED - i)])
+        for n, (re_part, im_part) in enumerate(results):
+            send_back[i, n, 0] = re_part.astype(BF)
+            send_back[i, n, 1] = (-im_part).astype(BF)
+        back_copy(i).start()
+
+    for i, crossed in enumerate(CROSSED_ORDER):
+        pl.when(has_prev & (chip != 4))(functools.partial(from_prev, i, i > 0))
+        pl.when(chip == 4)(functools.partial(from_prev, crossed, True))
+        pl.when(has_next & (chip != 3))(functools.partial(from_next, i, i > 0))
+        pl.when(chip == 3)(functools.partial(from_next, crossed, True))
 
     @pl.loop(0, 2 * DATES - UFIRST)
     def _(u):

time: 72.9 us -> 69.7 us (0.956)
  the two profiles are of different devices: /device:TPU:7 before, /device:TPU:36 now
where the time goes in v4:
time: 69.7 us; the launch traced here: 69.5 us
  Pallas kernels  67.2 us (96%)
  local copies, waits for them, and re-layouts  2.31 us (3%)
    pallas_call x1, Pallas kernels, on_device(): pl.pallas_call(kernel, out_shape=jax.ShapeDtypeStruct((DATES, 4, 2, LROWS...  67.2 us
    unnamed x1, local copies, waits for them, and re-layouts  2.31 us

profile of v4, /device:TPU:36, one launch (start us, length us, event | category | flops | bytes accessed | tf_op | source)
XLA Modules:
  0.0 69.5 jit_solution(10970049003650879787)
XLA Ops:
  0.0 67.2 %coherence_stack.1 = f32[8,4,2,16,192]{4,3,2,1,0:T(8,128)} custom-call(bf16[8,64,2,3840]{3,2,1,0:T(2,128)(2,1)} %raw.1, s32[8]{0:T(128)} %line_shift.1, s32[8]{0:T(128)} %line_phase.1, s32[8]{0:T(128)} %col_shift.1, s32[8]{0:T(128)} %col_phase.1, s32[4,8]{1,0:T(4,128)} %bitcast.1, f32[128]{0:T(128)} %constant.2.clone.table), custom_call_target="tpu_custom_call" | custom-call | tf_op jit(solution)/shard_map/coherence_stack/pallas_call | solution.py:594
  67.2 2.3 %copy.9 = f32[8,4,2,16,192]{4,3,2,1,0:T(8,128)} copy(f32[8,4,2,16,192]{4,3,2,1,0:T(8,128)} %coherence_stack.1) | data formatting | bytes 1572864

commit v5 on v4

--- a/solution.py
+++ b/solution.py
@@ -389,7 +389,7 @@
     def sums(x_at, others):
         count = len(others)
 
-        @pl.loop(0, HTILES)
+        @pl.loop(0, HTILES, unroll=5)
         def _(c):
             lanes = pl.ds(pl.multiple_of(c * 128, 128), 128)
             x = images[x_at, :, lanes]

time: 69.7 us -> 69.6 us (level)
  no operation moved by 1% of the time
where the time goes in v5:
time: 69.6 us; the launch traced here: 69.5 us
  Pallas kernels  67.1 us (96%)
  local copies, waits for them, and re-layouts  2.31 us (3%)
    pallas_call x1, Pallas kernels, on_device(): pl.pallas_call(kernel, out_shape=jax.ShapeDtypeStruct((DATES, 4, 2, LROWS...  67.1 us
    unnamed x1, local copies, waits for them, and re-layouts  2.31 us

profile of v5, /device:TPU:36, one launch (start us, length us, event | category | flops | bytes accessed | tf_op | source)
XLA Modules:
  0.0 69.5 jit_solution(15321034693694328360)
XLA Ops:
  0.0 67.1 %coherence_stack.1 = f32[8,4,2,16,192]{4,3,2,1,0:T(8,128)} custom-call(bf16[8,64,2,3840]{3,2,1,0:T(2,128)(2,1)} %raw.1, s32[8]{0:T(128)} %line_shift.1, s32[8]{0:T(128)} %line_phase.1, s32[8]{0:T(128)} %col_shift.1, s32[8]{0:T(128)} %col_phase.1, s32[4,8]{1,0:T(4,128)} %bitcast.1, f32[128]{0:T(128)} %constant.2.clone.table), custom_call_target="tpu_custom_call" | custom-call | tf_op jit(solution)/shard_map/coherence_stack/pallas_call | solution.py:594
  67.2 2.3 %copy.9 = f32[8,4,2,16,192]{4,3,2,1,0:T(8,128)} copy(f32[8,4,2,16,192]{4,3,2,1,0:T(8,128)} %coherence_stack.1) | data formatting | bytes 1572864
